TPU v7x, 256 devices: a whole 4x4x8 slice. The times are simulated.
256 devices in a mesh: row: 8 (over z), col: 32 (over x, y, core).
Axes of the slice: x: 4, y: 4, z: 8, core: 2. Of those that a mesh axis runs over, the one named last changes fastest.
Arguments:
- root_inv: bfloat16 [8192, 8192], P('row', 'col'), may hold values from -0.0625 to 0.0625
- panel: bfloat16 [8192, 4096], P(None, 'col'), may hold values from -1.5 to 1.5
- pattern: int32 [64, 32], replicated, may hold values 0 or 1
- child_diag: float32 [4096, 4096], P('row', 'col'), may hold values from -6 to 6
- owner: int32 [32], replicated, may hold values from 0 to 31, each once
Outputs:
- off_block: float32 [8192, 4096], P('row', 'col')
- diag_block: float32 [4096, 4096], P('row', 'col')
- owned_rows: bfloat16 [4096, 4096], P('col', 'row')
Inputs may be any that keep to these rules, and one draw needn't show every extreme that they name: owner is a permutation of the 32 block columns.
All inputs are finite; a program needn't handle non-finite values.
Results may differ from a plain program's by a relative error of at most 0.0039.
Values may be sent and summed in bfloat16 or wider, within the bound.
A program may use at most 128 MiB of HBM per device.

v0:
```python
import jax
import jax.numpy as jnp
from jax import lax
from jax.sharding import PartitionSpec as P


def on_device(root_inv, panel, pattern, child_diag, owner):
    col_index = lax.axis_index("col")
    row_index = lax.axis_index("row")
    block_size = panel.shape[0] // pattern.shape[0]
    local_blocks = panel.shape[1] // block_size
    pattern_cols = lax.dynamic_slice_in_dim(pattern, col_index * local_blocks, local_blocks, 1)
    expanded = jnp.repeat(jnp.repeat(pattern_cols, block_size, 0), block_size, 1)
    masked = jnp.where(expanded == 1, panel, jnp.zeros_like(panel))
    product = jnp.dot(
        lax.all_gather(root_inv, "col", axis=1, tiled=True),
        masked,
        preferred_element_type=jnp.float32,
    )
    off_block = -product
    off_wire = off_block.astype(jnp.bfloat16)
    slab_rows = root_inv.shape[0]
    own_slab = lax.dynamic_slice_in_dim(masked, row_index * slab_rows, slab_rows, 0)
    partial_terms = lax.dot_general(
        lax.all_gather(own_slab, "col", axis=1, tiled=True),
        off_wire,
        (((0,), (0,)), ((), ())),
        preferred_element_type=jnp.float32,
    )
    summed = lax.psum_scatter(partial_terms, "row", scatter_dimension=0, tiled=True)
    diag_block = child_diag - summed
    diag_wire = diag_block.astype(jnp.bfloat16)
    height = diag_wire.shape[0]
    flipped = diag_wire.reshape(height, local_blocks, block_size).transpose(1, 2, 0)
    my_owners = lax.dynamic_slice_in_dim(owner, col_index * local_blocks, local_blocks, 0)
    everything = lax.all_gather(flipped, "col", axis=0, tiled=True)
    select = (my_owners[:, None] == jnp.arange(everything.shape[0])[None, :]).astype(jnp.bfloat16)
    picked = jnp.einsum("kj,jbn->kbn", select, everything, preferred_element_type=jnp.float32)
    owned_rows = picked.astype(jnp.bfloat16).reshape(local_blocks * block_size, height)
    return (off_block, diag_block, owned_rows)


def solution(mesh):
    placed = (P("row", "col"), P(None, "col"), P(), P("row", "col"), P())
    return jax.shard_map(
        on_device,
        mesh=mesh,
        in_specs=placed,
        out_specs=(P("row", "col"), P("row", "col"), P("col", "row")),
        check_vma=False,
    )
```

profile of v0, /device:TPU:1, one launch (start us, length us, event | category | flops | bytes accessed | tf_op | source)
XLA Modules:
  0.0 283.3 jit_solution(7354654240620762838)
XLA Ops:
  7.2 0.0 all-gather.4.cloned.1.call-start
  7.2 0.7 all-gather.4.cloned.1.call-update
  7.9 0.0 all-gather.6.cloned.1.call-start
  8.0 0.7 compare_bitcast_fusion
  8.7 0.1 broadcast_bitcast_fusion
  8.7 5.8 %broadcast_select_fusion = bf16[8192,128]{1,0:T(8,128)(2,1)S(1)} fusion(bf16[8192,128]{1,0:T(8,128)(2,1)} %param.6, pred[8192]{0:T(1024)(128)(4,1)S(1)} %broadcast_bitcast_fusion), kind=kLoop, calls=%fused_computation.2 | loop fusion | flops 1048576 | bytes 4202496 | tf_op jit(solution)/shard_map/jit(_where)/select_n | solution.py:14
  14.6 0.7 constant_dynamic-slice_fusion
  15.3 0.0 all-gather.6.cloned.1.call-update
  15.3 0.0 reduce-scatter.2.cloned.1.call-start
  15.4 85.4 %all-gather.4.cloned.1.call-done = bf16[1024,8192]{1,0:T(8,128)(2,1)} async-done(((bf16[1024,256]{1,0:T(8,128)(2,1)}), bf16[1024,8192]{1,0:T(8,128)(2,1)}) %all-gather.4.cloned.1.call-update) | async-done | bytes 16777232 | tf_op jit(solution)/shard_map/all_gather | solution.py:16
  100.8 11.5 %fusion.2 = f32[1024,128]{0,1:T(8,128)S(1)} fusion(bf16[8192,128]{1,0:T(8,128)(2,1)S(1)} %broadcast_select_fusion, bf16[1024,8192]{1,0:T(8,128)(2,1)} %all-gather.4.cloned.1.call-done), kind=kOutput, calls=%fused_computation.4 | convolution fusion | flops 2147614720 | bytes 19398656 | tf_op jit(solution)/shard_map/dot_general | solution.py:15
  112.3 0.0 copy-start
  112.3 0.0 copy-start.1
  112.3 56.3 %all-gather.6.cloned.1.call-done = bf16[1024,4096]{1,0:T(8,128)(2,1)} async-done(((bf16[1024,128]{1,0:T(8,128)(2,1)}), bf16[1024,4096]{1,0:T(8,128)(2,1)}) %all-gather.6.cloned.1.call-update) | async-done | bytes 8388624 | tf_op jit(solution)/shard_map/all_gather | solution.py:25
  168.6 7.1 %fusion.3 = f32[4096,128]{1,0:T(8,128)} fusion(bf16[1024,4096]{1,0:T(8,128)(2,1)} %all-gather.6.cloned.1.call-done, f32[1024,128]{0,1:T(8,128)S(1)} %fusion.2), kind=kOutput, calls=%fused_computation.6 | convolution fusion | flops 1073872896 | bytes 11010048 | tf_op jit(solution)/shard_map/dot_general | solution.py:24
  175.7 0.0 reduce-scatter.2.cloned.1.call-update
  175.7 0.0 all-gather.8.cloned.1.call-start
  175.8 37.5 %reduce-scatter.2.cloned.1.call-done = f32[512,128]{1,0:T(8,128)} async-done(((f32[4096,128]{1,0:T(8,128)}), f32[512,128]{1,0:T(8,128)}) %reduce-scatter.2.cloned.1.call-update) | async-done | bytes 262160 | tf_op jit(solution)/shard_map/reduce_scatter | solution.py:30
  213.3 0.0 copy-done
  213.3 1.7 convert_bitcast_fusion
  215.0 0.8 copy.9
  215.7 0.0 all-gather.8.cloned.1.call-update
  215.8 0.0 copy-done.1
  215.8 0.7 dynamic_slice.11
  216.4 1.0 copy.10
  217.4 53.3 %all-gather.8.cloned.1.call-done = bf16[32,128,512]{2,1,0:T(8,128)(2,1)} async-done(((bf16[1,128,512]{2,1,0:T(8,128)(2,1)}), bf16[32,128,512]{2,1,0:T(8,128)(2,1)}) %all-gather.8.cloned.1.call-update) | async-done | bytes 4194320 | tf_op jit(solution)/shard_map/all_gather | solution.py:36
  270.7 5.3 %fusion = bf16[1,128,512]{2,0,1:T(2,128)(2,1)S(1)} fusion(bf16[32,128,512]{2,1,0:T(8,128)(2,1)} %all-gather.8.cloned.1.call-done, s32[]{:T(128)} %bitcast.3), kind=kOutput, calls=%fused_computation | convolution fusion | flops 4194336 | bytes 4325380 | tf_op jit(solution)/shard_map/kj,jbn->kbn/dot_general | solution.py:38
  276.0 0.7 copy.16
Async XLA Ops:
  7.2 93.6 %all-gather.4.cloned.1.call-start = ((), (), s32[]{:S(2)}) async-start(), calls=%async_computation.1 | async-start | bytes 17301504 | tf_op jit(solution)/shard_map/all_gather | solution.py:16
  7.9 160.7 %all-gather.6.cloned.1.call-start = ((), (), s32[]{:S(2)}) async-start(), calls=%async_computation.2 | async-start | bytes 8650752 | tf_op jit(solution)/shard_map/all_gather | solution.py:25
  15.3 198.0 %reduce-scatter.2.cloned.1.call-start = ((), (), s32[]{:S(2)}) async-start(), calls=%async_computation.3 | async-start | bytes 2359296 | tf_op jit(solution)/shard_map/reduce_scatter | solution.py:30
  112.3 101.0 %copy-start = (f32[512,128]{1,0:T(8,128)S(1)}, f32[512,128]{1,0:T(8,128)}, u32[]{:S(2)}) copy-start(f32[512,128]{1,0:T(8,128)} %param.8) | copy-start | bytes 786436
  112.3 103.5 %copy-start.1 = (s32[32]{0:T(128)S(1)}, s32[32]{0:T(128)}, u32[]{:S(2)}) copy-start(s32[32]{0:T(128)} %param.9) | copy-start | bytes 388
  175.7 95.0 %all-gather.8.cloned.1.call-start = ((), (), s32[]{:S(2)}) async-start(), calls=%async_computation.4 | async-start | bytes 4325376 | tf_op jit(solution)/shard_map/all_gather | solution.py:36
Sparse Core Ops, SparseCore 0:
  10.5 90.2 all-gather.3
  103.8 64.7 all-gather.5
  175.8 37.3 reduce-scatter.1
  216.3 54.4 all-gather.7
where the time goes:
time: 284 us; the launch traced here: 283 us
  waiting for transfers between devices  233 us (82%)
  matrix products  23.9 us (8%)
  between operations  13.8 us (5%)
  other arithmetic  8.21 us (3%)
  local copies, waits for them, and re-layouts  3.93 us (1%)
    all_gather x1, waiting for transfers between devices, on_device(): lax.all_gather(root_inv, 'col', axis=1, tiled=True)  85.4 us
    all_gather x1, waiting for transfers between devices, on_device(): lax.all_gather(own_slab, 'col', axis=1, tiled=True)  56.3 us
    all_gather x1, waiting for transfers between devices, on_device(): everything = lax.all_gather(flipped, 'col', axis=0, tiled=True)  53.3 us
    reduce_scatter x1, waiting for transfers between devices, on_device(): lax.psum_scatter(partial_terms, 'row', scatter_dimension=0, tiled=True)  37.5 us
    dot_general x1, matrix products, on_device(): jnp.dot(lax.all_gather(root_inv, 'col', axis=1, tiled=True), masked, pref...  11.5 us
    dot_general x1, matrix products, on_device(): lax.dot_general(lax.all_gather(own_slab, 'col', axis=1, tiled=True), off_...  7.1 us
    select_n x1, other arithmetic, on_device(): masked = jnp.where(expanded == 1, panel, jnp.zeros_like(panel))  5.82 us
  transfers between devices with their start and end apart: 4, of which 4 were waited for; matrix products, arithmetic and copies ran while one was open for 7% of the time, Pallas kernels for 0%

commit v1 on v0

v1 whole, which is shorter than its diff:
```python
import functools

import jax
import jax.numpy as jnp
from jax import lax
from jax.experimental import pallas as pl
from jax.experimental.pallas import tpu as pltpu
from jax.sharding import PartitionSpec as P

MESH = pl.DeviceIdType.MESH
BF = jnp.bfloat16
F32 = jnp.float32

NX, NY, NZ = 4, 4, 8
Z_STEPS = 2
DIRECT = (0, 3, 4, 5)


def at(start, size):
    return pl.ds(pl.multiple_of(start, size), size)


class Links:
    def __init__(self, send_sems, recv_sems):
        self.send_sems, self.recv_sems = send_sems, recv_sems
        self.count = 0
        self.started = []

    def send(self, src, dst, device):
        index = self.count
        self.count += 1
        copy = pltpu.make_async_remote_copy(
            src_ref=src,
            dst_ref=dst,
            send_sem=self.send_sems.at[index],
            recv_sem=self.recv_sems.at[index],
            device_id=device,
            device_id_type=MESH,
        )
        copy.start()
        self.started.append(copy)
        return copy

    def drain(self):
        for copy in self.started:
            copy.wait_send()


N_LINKS = 11 + 9 + 3 + 3 * len(DIRECT) + 2 * Z_STEPS + 48 + 32 + 12 + 7


def kernel(
    root, panel, pattern, child, owner,
    off_out, diag_out, own_out,
    r_all, panel_v, m_send, m_all, mr_all, child_all,
    prod, y_send, y_recv, o_all, d_all, z_send, z_recv, s_fin, e_all, w_all,
    sib_send, sib_recv, comb, x_send, x_recv,
    send_sems, recv_sems, e_recv, e_own_send, local_sems,
):
    z = lax.axis_index("row")
    c = lax.axis_index("col")
    h = c % 2
    y = (c // 2) % NY
    x = c // (2 * NY)

    def device(xx, yy, hh, zz):
        return (zz, (xx * NY + yy) * 2 + hh)

    def wrap(value, size):
        return (value + size) % size

    x_up, x_dn, x_far = wrap(x + 1, NX), wrap(x - 1, NX), wrap(x + 2, NX)
    y_up, y_dn, y_far = wrap(y + 1, NY), wrap(y - 1, NY), wrap(y + 2, NY)
    z_up, z_dn = wrap(z + 1, NZ), wrap(z - 1, NZ)
    z_pair = z + 1 - 2 * (z % 2)
    sib = device(x, y, 1 - h, z)
    to_xu, to_xd = device(x_up, y, h, z), device(x_dn, y, h, z)
    to_yu, to_yd = device(x, y_up, h, z), device(x, y_dn, h, z)
    to_zu, to_zd = device(x, y, h, z_up), device(x, y, h, z_dn)

    links = Links(send_sems, recv_sems)
    send = links.send

    seg_own = x * 2 + h
    own_r = pltpu.make_async_copy(root, r_all.at[seg_own], local_sems.at[0])
    own_r.start()
    own_panel = pltpu.make_async_copy(panel, panel_v, local_sems.at[1])
    own_panel.start()
    own_child = pltpu.make_async_copy(child, child_all.at[y], local_sems.at[2])
    own_child.start()

    barrier = pltpu.get_barrier_semaphore()
    peers = [sib, to_xu, to_xd, to_zu, to_zd]
    for k in range(1, NY):
        peers.append(device(x, wrap(y + k, NY), h, z))
        peers.append(device(x, wrap(y + k, NY), h, z_pair))
    for peer in peers:
        pl.semaphore_signal(barrier, inc=1, device_id=peer, device_id_type=MESH)
    pl.semaphore_wait(barrier, len(peers))

    top, low = pl.ds(0, 512), pl.ds(512, 512)
    r0 = send(root.at[top], r_all.at[seg_own, top], to_xu)
    r1 = send(root.at[low], r_all.at[seg_own, low], to_xd)
    r2 = send(root.at[low], r_all.at[seg_own, low], to_xu)
    r3 = send(root.at[top], r_all.at[seg_own, top], to_xd)
    r6 = send(root, r_all.at[seg_own], sib)

    own_panel.wait()

    def mask_into(dst_of, first_row, blocks):
        def body(i, carry):
            row = first_row + i * 128
            on = pattern[row // 128, c].astype(F32)
            value = panel_v[at(row, 128), :].astype(F32) * on
            dst_of(i, value)
            return carry

        lax.fori_loop(0, blocks, body, 0)

    def segment_row(s, yy):
        return (((s // 2) * NY + yy) * 2 + s % 2) * 256

    m_copies = {}
    for i, d in enumerate(DIRECT):
        s = (z + d) % NZ
        for k in range(1, NY):

            def put(b, value, i=i, k=k):
                m_send[i, k - 1, at(b * 128, 128), :] = value.astype(BF)

            mask_into(put, segment_row(s, (y + k) % NY), 2)
            m_copies[i, k] = send(
                m_send.at[i, k - 1],
                m_all.at[NY - k, at(s * 256, 256)],
                device(x, (y + k) % NY, h, z),
            )

    child_copies = [
        send(child, child_all.at[y], device(x, (y + k) % NY, h, z)) for k in range(1, NY)
    ]

    def own_segment(s, carry):
        def put(b, value):
            m_all[0, at(s * 256 + b * 128, 128), :] = value.astype(BF)

        mask_into(put, segment_row(s, y), 2)
        return carry

    lax.fori_loop(0, 8, own_segment, 0)

    def put_transposed(b, value):
        mr_all[at(seg_own * 128, 128), at(b * 128, 128)] = value.T.astype(BF)

    mask_into(put_transposed, z * 1024, 8)

    def m_slot(s):
        return m_all.at[pl.ds(1, NY - 1), at(s * 256, 256)]

    for k in range(1, NY):
        m_copies[0, k].wait_recv()
    up = send(m_slot(z), m_slot(z), to_zu)
    down = send(m_slot(z), m_slot(z), to_zd)

    r0.wait_recv()
    seg_dn, seg_up, seg_far = x_dn * 2 + h, x_up * 2 + h, x_far * 2 + h
    r4 = send(r_all.at[seg_dn, top], r_all.at[seg_dn, top], to_xu)
    r1.wait_recv()
    r5 = send(r_all.at[seg_up, low], r_all.at[seg_up, low], to_xd)

    for step in range(1, Z_STEPS):
        up.wait_recv()
        s = wrap(z - step, NZ)
        up = send(m_slot(s), m_slot(s), to_zu)
        down.wait_recv()
        s = wrap(z + step, NZ)
        down = send(m_slot(s), m_slot(s), to_zd)

    r2.wait_recv()
    r7 = send(r_all.at[seg_dn], r_all.at[seg_dn], sib)
    r3.wait_recv()
    r8 = send(r_all.at[seg_up], r_all.at[seg_up], sib)

    def mr_rows(s):
        return mr_all.at[at(s * 128, 128)]

    def mr_half(s, half):
        return mr_all.at[at(s * 128 + half * 64, 64)]

    t0 = send(mr_rows(seg_own), mr_rows(seg_own), to_xu)
    t1 = send(mr_rows(seg_own), mr_rows(seg_own), to_xd)
    t4 = send(mr_rows(seg_own), mr_rows(seg_own), sib)

    up.wait_recv()
    down.wait_recv()
    for i in range(1, len(DIRECT)):
        for k in range(1, NY):
            m_copies[i, k].wait_recv()
    own_r.wait()
    r6.wait_recv()
    r7.wait_recv()
    r8.wait_recv()

    def m_of(chunk, s):
        return m_all[(chunk - y + NY) % NY, at(s * 256, 256), :]

    def first_product(i, carry):
        chunk, rows = i // 4, at((i % 4) * 256, 256)
        total = None
        for xx in (x, x_dn, x_up):
            for hh in range(2):
                s = xx * 2 + hh
                term = jnp.dot(r_all[s, rows, :], m_of(chunk, s), preferred_element_type=F32)
                total = term if total is None else total + term
        prod[chunk, rows, :] = total
        return carry

    lax.fori_loop(0, 16, first_product, 0)

    r4.wait_recv()
    r9 = send(r_all.at[seg_far, top], r_all.at[seg_far, top], sib)
    r5.wait_recv()
    r10 = send(r_all.at[seg_far, low], r_all.at[seg_far, low], sib)

    t0.wait_recv()
    t2 = send(mr_half(seg_dn, 0), mr_half(seg_dn, 0), to_xu)
    t5 = send(mr_rows(seg_dn), mr_rows(seg_dn), sib)
    t1.wait_recv()
    t3 = send(mr_half(seg_up, 1), mr_half(seg_up, 1), to_xd)
    t6 = send(mr_rows(seg_up), mr_rows(seg_up), sib)

    r9.wait_recv()
    r10.wait_recv()

    ycopy, zcopy, ecopy = {}, {}, {}

    def finish(chunk, quarter):
        rows = at(quarter * 256, 256)
        total = prod[chunk, rows, :]
        for hh in range(2):
            s = x_far * 2 + hh
            total += jnp.dot(r_all[s, rows, :], m_of(chunk, s), preferred_element_type=F32)
        prod[chunk, rows, :] = total

    def half_rows(quarter, half):
        return at(quarter * 256 + half * 128, 128)

    def y_out(chunk, slot, value, to):
        y_send[chunk, slot] = value.astype(BF)
        ycopy[chunk, slot] = send(y_send.at[chunk, slot], y_recv.at[chunk, slot], to)

    def stage_a(chunk):
        finish(chunk, y_far)
        y_out(chunk, 0, prod[chunk, half_rows(y_far, 0), :], to_yu)
        y_out(chunk, 1, prod[chunk, half_rows(y_far, 1), :], to_yd)
        finish(chunk, y_up)
        y_out(chunk, 2, prod[chunk, half_rows(y_up, 1), :], to_yu)
        finish(chunk, y_dn)
        y_out(chunk, 3, prod[chunk, half_rows(y_dn, 0), :], to_yd)
        finish(chunk, y)

    def stage_b(chunk):
        ycopy[chunk, 0].wait_recv()
        value = prod[chunk, half_rows(y_up, 0), :] + y_recv[chunk, 0].astype(F32)
        y_out(chunk, 4, value, to_yu)
        ycopy[chunk, 1].wait_recv()
        value = prod[chunk, half_rows(y_dn, 1), :] + y_recv[chunk, 1].astype(F32)
        y_out(chunk, 5, value, to_yd)

    def o_copy(chunk, slot, quarter, half, to):
        ref = o_all.at[chunk, half_rows(quarter, half)]
        ycopy[chunk, slot] = send(ref, ref, to)

    def stage_c(chunk):
        ycopy[chunk, 3].wait_recv()
        ycopy[chunk, 4].wait_recv()
        o_all[chunk, half_rows(y, 0), :] = (
            prod[chunk, half_rows(y, 0), :] + y_recv[chunk, 3].astype(F32) + y_recv[chunk, 4].astype(F32)
        ).astype(BF)
        o_copy(chunk, 6, y, 0, to_yu)
        ycopy[chunk, 2].wait_recv()
        ycopy[chunk, 5].wait_recv()
        o_all[chunk, half_rows(y, 1), :] = (
            prod[chunk, half_rows(y, 1), :] + y_recv[chunk, 2].astype(F32) + y_recv[chunk, 5].astype(F32)
        ).astype(BF)
        o_copy(chunk, 7, y, 1, to_yd)
        o_copy(chunk, 8, y, 1, to_yu)
        o_copy(chunk, 9, y, 0, to_yd)

    def stage_d(chunk):
        ycopy[chunk, 6].wait_recv()
        o_copy(chunk, 10, y_dn, 0, to_yu)
        ycopy[chunk, 7].wait_recv()
        o_copy(chunk, 11, y_up, 1, to_yd)

    def z_out(chunk, slot, size, value, to):
        z_send[chunk, slot, pl.ds(0, size), :] = value
        zcopy[chunk, slot] = send(
            z_send.at[chunk, slot, pl.ds(0, size)], z_recv.at[chunk, slot, pl.ds(0, size)], to
        )

    def stage_e(chunk):
        for slot in (8, 9, 10, 11):
            ycopy[chunk, slot].wait_recv()

        def body(i, carry):
            rows = at(i * 256, 256)
            d_all[chunk, rows, :] = jnp.dot(mr_all[rows, :], o_all[chunk], preferred_element_type=F32)
            return carry

        lax.fori_loop(0, 4, body, 0)
        far = (z + 4) % NZ
        z_out(chunk, 0, 64, d_all[chunk, at(far * 128, 64), :], to_zu)
        z_out(chunk, 4, 64, d_all[chunk, at(far * 128 + 64, 64), :], to_zd)

    def stage_f(chunk, step):
        zcopy[chunk, step - 1].wait_recv()
        base = ((z + 4 - step) % NZ) * 128
        if step == 1:
            value = jnp.concatenate(
                [
                    d_all[chunk, at(base, 64), :] + z_recv[chunk, 0, pl.ds(0, 64), :],
                    d_all[chunk, at(base + 64, 64), :],
                ],
                axis=0,
            )
        else:
            value = d_all[chunk, at(base, 128), :] + z_recv[chunk, step - 1]
        z_out(chunk, step, 128, value, to_zu)
        zcopy[chunk, 4 + step - 1].wait_recv()
        base = ((z + 4 + step) % NZ) * 128
        if step == 1:
            value = jnp.concatenate(
                [
                    d_all[chunk, at(base, 64), :],
                    d_all[chunk, at(base + 64, 64), :] + z_recv[chunk, 4, pl.ds(0, 64), :],
                ],
                axis=0,
            )
        else:
            value = d_all[chunk, at(base, 128), :] + z_recv[chunk, 4 + step - 1]
        z_out(chunk, 4 + step, 128, value, to_zd)

    keeps = (z % 2) == (y // 2)
    e_z = 2 * (z // 2) + y // 2
    e_slot = 2 * (y % 2) + z % 2

    def e_dst(chunk):
        return e_all.at[chunk, at(e_slot * 128, 128)]

    def e_here(chunk):
        return pltpu.make_async_copy(s_fin.at[chunk], e_dst(chunk), e_recv.at[chunk, e_slot])

    def e_there(chunk):
        return pltpu.make_async_remote_copy(
            src_ref=s_fin.at[chunk],
            dst_ref=e_dst(chunk),
            send_sem=e_own_send.at[chunk, 0],
            recv_sem=e_recv.at[chunk, e_slot],
            device_id=device(x, y, h, z_pair),
            device_id_type=MESH,
        )

    def stage_g(chunk):
        zcopy[chunk, 3].wait_recv()
        zcopy[chunk, 7].wait_recv()
        s_fin[chunk] = (
            d_all[chunk, at(z * 128, 128), :] + z_recv[chunk, 3] + z_recv[chunk, 7]
        )
        for k in range(1, NY):
            copy = pltpu.make_async_remote_copy(
                src_ref=s_fin.at[chunk],
                dst_ref=e_dst(chunk),
                send_sem=e_own_send.at[chunk, k],
                recv_sem=e_recv.at[chunk, e_slot],
                device_id=device(x, (y + k) % NY, h, e_z),
                device_id_type=MESH,
            )
            copy.start()
            links.started.append(copy)

        @pl.when(keeps)
        def _():
            e_here(chunk).start()

        @pl.when(jnp.logical_not(keeps))
        def _():
            e_there(chunk).start()

    def stage_h(chunk):
        for slot in range(4):
            ref = e_all.at[chunk, pl.ds(slot * 128, 128)]
            pltpu.make_async_copy(ref, ref, e_recv.at[chunk, slot]).wait()
        w_all[chunk] = (child_all[chunk] + e_all[chunk]).astype(BF)

    t2_waited = False
    stages = [
        stage_a, stage_b, stage_c, stage_d, stage_e,
        lambda ch: stage_f(ch, 1), lambda ch: stage_f(ch, 2), lambda ch: stage_f(ch, 3),
        stage_g, stage_h,
    ]
    for step in range(len(stages) + NY - 1):
        if step == 3:
            t2.wait_recv()
            t3.wait_recv()
            t7 = send(mr_rows(seg_far), mr_rows(seg_far), sib)
            own_child.wait()
            for copy in child_copies:
                copy.wait_recv()
        if step == 4:
            for copy in (t4, t5, t6, t7):
                copy.wait_recv()
        for chunk in range(NY):
            stage = step - chunk
            if 0 <= stage < len(stages):
                stages[stage](chunk)

    off_out[...] = o_all[y]
    diag_out[...] = child_all[y] + e_all[y]

    def candidate(xx, hh):
        t = owner[(xx * NY + y) * 2 + hh]
        on = jnp.logical_and(t // (2 * NY) == x, t % 2 == h).astype(F32)
        return w_all[(t // 2) % NY].astype(F32) * on

    for xx in range(NX):
        sib_send[xx] = candidate(xx, 1 - h).astype(BF)
    sib_copy = send(sib_send, sib_recv, sib)
    for xx in range(NX):
        comb[xx] = candidate(xx, h)
    sib_copy.wait_recv()
    for xx in range(NX):
        comb[xx] = comb[xx] + sib_recv[xx].astype(F32)

    xcopy = {}

    def x_out(slot, value, to):
        x_send[slot] = value.astype(BF)
        xcopy[slot] = send(x_send.at[slot], x_recv.at[slot], to)

    first, second = pl.ds(0, 256), pl.ds(256, 256)
    x_out(0, comb[x_far, first, :], to_xu)
    x_out(1, comb[x_far, second, :], to_xd)
    x_out(2, comb[x_up, second, :], to_xu)
    x_out(3, comb[x_dn, first, :], to_xd)
    xcopy[0].wait_recv()
    x_out(4, comb[x_up, first, :] + x_recv[0].astype(F32), to_xu)
    xcopy[1].wait_recv()
    x_out(5, comb[x_dn, second, :] + x_recv[1].astype(F32), to_xd)
    for slot in (2, 3, 4, 5):
        xcopy[slot].wait_recv()
    own_out[first, :] = (comb[x, first, :] + x_recv[3].astype(F32) + x_recv[4].astype(F32)).astype(BF)
    own_out[second, :] = (comb[x, second, :] + x_recv[2].astype(F32) + x_recv[5].astype(F32)).astype(BF)

    links.drain()
    for chunk in range(NY):

        @pl.when(jnp.logical_not(keeps))
        def _(chunk=chunk):
            e_there(chunk).wait_send()


def on_device(root_inv, panel, pattern, child_diag, owner):
    vmem = pl.BlockSpec(memory_space=pltpu.VMEM)
    smem = pl.BlockSpec(memory_space=pltpu.SMEM)
    hbm = pl.BlockSpec(memory_space=pl.ANY)
    off, diag, own = pl.pallas_call(
        kernel,
        out_shape=(
            jax.ShapeDtypeStruct((1024, 128), BF),
            jax.ShapeDtypeStruct((512, 128), F32),
            jax.ShapeDtypeStruct((512, 128), BF),
        ),
        in_specs=[hbm, hbm, smem, hbm, smem],
        out_specs=(vmem, vmem, vmem),
        scratch_shapes=[
            pltpu.VMEM((8, 1024, 256), BF),
            pltpu.VMEM((8192, 128), BF),
            pltpu.VMEM((len(DIRECT), NY - 1, 256, 128), BF),
            pltpu.VMEM((NY, 2048, 128), BF),
            pltpu.VMEM((1024, 1024), BF),
            pltpu.VMEM((NY, 512, 128), F32),
            pltpu.VMEM((NY, 1024, 128), F32),
            pltpu.VMEM((NY, 6, 128, 128), BF),
            pltpu.VMEM((NY, 6, 128, 128), BF),
            pltpu.VMEM((NY, 1024, 128), BF),
            pltpu.VMEM((NY, 1024, 128), F32),
            pltpu.VMEM((NY, 8, 128, 128), F32),
            pltpu.VMEM((NY, 8, 128, 128), F32),
            pltpu.VMEM((NY, 128, 128), F32),
            pltpu.VMEM((NY, 512, 128), F32),
            pltpu.VMEM((NY, 512, 128), BF),
            pltpu.VMEM((NX, 512, 128), BF),
            pltpu.VMEM((NX, 512, 128), BF),
            pltpu.VMEM((NX, 512, 128), F32),
            pltpu.VMEM((6, 256, 128), BF),
            pltpu.VMEM((6, 256, 128), BF),
            pltpu.SemaphoreType.DMA((N_LINKS,)),
            pltpu.SemaphoreType.DMA((N_LINKS,)),
            pltpu.SemaphoreType.DMA((NY, 4)),
            pltpu.SemaphoreType.DMA((NY, 4)),
            pltpu.SemaphoreType.DMA((3,)),
        ],
        compiler_params=pltpu.CompilerParams(
            collective_id=0, has_side_effects=True, vmem_limit_bytes=48 * 1024 * 1024
        ),
    )(root_inv, panel, pattern, child_diag, owner)
    return -off.astype(F32), diag, own.T


def solution(mesh):
    placed = (P("row", "col"), P(None, "col"), P(), P("row", "col"), P())
    return jax.shard_map(
        on_device,
        mesh=mesh,
        in_specs=placed,
        out_specs=(P("row", "col"), P("row", "col"), P("col", "row")),
        check_vma=False,
    )
```

time: 284 us -> 119 us (0.42)
  waiting for transfers between devices: 233 us -> 0 us
  Pallas kernels: 0 us -> 111 us
  matrix products: 23.9 us -> 0 us
  between operations: 13.8 us -> 0.65 us
  other arithmetic: 8.21 us -> 0.83 us
    all_gather x3 -> x0, waiting for transfers between devices: 195 us -> none  [the longest x1 85.4 us: on_device(): lax.all_gather(root_inv, 'col', axis=1, tiled=True)]
    pallas_call x0 -> x1, Pallas kernels: none -> 111 us  [on_device(): pl.pallas_call(kernel, out_shape=(jax.ShapeDtypeStruct((1024, 128), BF),...]
    reduce_scatter x1 -> x0, waiting for transfers between devices: 37.5 us -> none  [on_device(): lax.psum_scatter(partial_terms, 'row', scatter_dimension=0, tiled=True)]
    dot_general x3 -> x0, matrix products: 23.9 us -> none  [the longest x1 11.5 us: on_device(): jnp.dot(lax.all_gather(root_inv, 'col', axis=1, tiled=True), masked, pref...]
    select_n x1 -> x0, other arithmetic: 5.82 us -> none  [on_device(): masked = jnp.where(expanded == 1, panel, jnp.zeros_like(panel))]
    unnamed x5 -> x11, local copies, waits for them, and re-layouts: 1.01 us -> 6.51 us
  transfers between devices with their start and end apart: 4 -> 0, of which waited for: 4 -> 0; matrix products, arithmetic and copies ran while one was open for 7% -> 0% of each run, Pallas kernels for 0% -> 0%
where the time goes in v1:
time: 119 us
  Pallas kernels  111 us (93%)
  local copies, waits for them, and re-layouts  6.51 us (5%)
    pallas_call x1, Pallas kernels, on_device(): pl.pallas_call(kernel, out_shape=(jax.ShapeDtypeStruct((1024, 128), BF),...  111 us
    unnamed x11, local copies, waits for them, and re-layouts  6.51 us

profile of v1, /device:TPU:1, one launch (start us, length us, event | category | flops | bytes accessed | tf_op | source)
XLA Modules:
  0.0 118.7 jit_solution(5261840886849098914)
XLA Ops:
  0.6 0.8 copy.8.pattern
  1.4 0.0 copy-start
  1.4 1.6 %copy-done = bf16[8192,128]{1,0:T(8,128)(2,1)S(1)} copy-done((bf16[8192,128]{1,0:T(8,128)(2,1)S(1)}, bf16[8192,128]{1,0:T(8,128)(2,1)}, u32[]{:S(2)}) %copy-start) | copy-done | bytes 2097176
  3.0 0.0 copy-start.1
  3.0 1.0 copy-done.1
  4.1 0.0 copy-start.2
  4.1 0.9 copy-done.2
  5.0 0.0 copy-start.3
  5.0 0.7 copy-done.3
  5.7 110.7 %shard_map.76 = (bf16[1024,128]{1,0:T(8,128)(2,1)S(1)}, f32[512,128]{1,0:T(8,128)S(1)}, bf16[512,128]{1,0:T(8,128)(2,1)S(1)}) custom-call(bf16[1024,256]{1,0:T(8,128)(2,1)S(1)} %copy-done.1, bf16[8192,128]{1,0:T(8,128)(2,1)S(1)} %copy-done, s32[64,32]{1,0:T(8,128)S(1)} %copy.8.pattern, f32[512,128]{1,0:T(8,128)S(1)} %copy-done.2, s32[32]{0:T(128)S(1)} %copy-done.3), custom_call_target="tpu_custom_call" | custom-call | tf_op jit(solution)/shard_map/pallas_call | solution.py:466
  116.4 0.8 copy.9
  117.2 0.8 convert_negate_fusion
  118.0 0.7 copy.11
Async XLA Ops:
  1.4 1.6 %copy-start = (bf16[8192,128]{1,0:T(8,128)(2,1)S(1)}, bf16[8192,128]{1,0:T(8,128)(2,1)}, u32[]{:S(2)}) copy-start(bf16[8192,128]{1,0:T(8,128)(2,1)} %panel.1) | copy-start | bytes 6291460
  3.0 1.0 copy-start.1
  4.1 0.9 copy-start.2
  5.0 0.7 copy-start.3

commit v2 on v1

v2 whole, which is shorter than its diff:
```python
import functools

import jax
import jax.numpy as jnp
from jax import lax
from jax.experimental import pallas as pl
from jax.experimental.pallas import tpu as pltpu
from jax.sharding import PartitionSpec as P

MESH = pl.DeviceIdType.MESH
BF = jnp.bfloat16
F32 = jnp.float32

NX, NY, NZ = 4, 4, 8
Z_STEPS = 2
DIRECT = (0, 3, 4, 5)


def at(start, size):
    return pl.ds(pl.multiple_of(start, size), size)


class Links:
    def __init__(self, send_sems, recv_sems):
        self.send_sems, self.recv_sems = send_sems, recv_sems
        self.count = 0
        self.started = []

    def send(self, src, dst, device):
        index = self.count
        self.count += 1
        copy = pltpu.make_async_remote_copy(
            src_ref=src,
            dst_ref=dst,
            send_sem=self.send_sems.at[index],
            recv_sem=self.recv_sems.at[index],
            device_id=device,
            device_id_type=MESH,
        )
        copy.start()
        self.started.append(copy)
        return copy

    def drain(self):
        for copy in self.started:
            copy.wait_send()


N_LINKS = 11 + 8 + 3 + 3 * len(DIRECT) + 4 * Z_STEPS + NY * (12 + 8 + 3 + 1) + 3


def kernel(
    root, panel, pattern, child, owner,
    off_out, diag_out, own_out,
    r_all, panel_v, m_send, m_all, mr_own, mr_all, child_v, child_all,
    prod, p_send, y_send, y_recv, o_all, d_all, z_send, z_recv, z_last_send, z_last_recv,
    d_send, d_here, w_all, x_send, x_recv,
    send_sems, recv_sems, swap_sems, d_send_sems, d_recv_sems, local_sems,
):
    z = lax.axis_index("row")
    c = lax.axis_index("col")
    h = c % 2
    y = (c // 2) % NY
    x = c // (2 * NY)

    def device(xx, yy, hh, zz):
        return (zz, (xx * NY + yy) * 2 + hh)

    def wrap(value, size):
        return (value + size) % size

    x_up, x_dn, x_far = wrap(x + 1, NX), wrap(x - 1, NX), wrap(x + 2, NX)
    y_up, y_dn, y_far = wrap(y + 1, NY), wrap(y - 1, NY), wrap(y + 2, NY)
    z_up, z_dn = wrap(z + 1, NZ), wrap(z - 1, NZ)
    sib = device(x, y, 1 - h, z)
    to_xu, to_xd = device(x_up, y, h, z), device(x_dn, y, h, z)
    to_yu, to_yd = device(x, y_up, h, z), device(x, y_dn, h, z)
    to_zu, to_zd = device(x, y, h, z_up), device(x, y, h, z_dn)

    links = Links(send_sems, recv_sems)
    send = links.send

    seg_own = x * 2 + h
    own_r = pltpu.make_async_copy(root, r_all.at[seg_own], local_sems.at[0])
    own_r.start()
    own_panel = pltpu.make_async_copy(panel, panel_v, local_sems.at[1])
    own_panel.start()
    own_child = pltpu.make_async_copy(child, child_v, local_sems.at[2])
    own_child.start()

    barrier = pltpu.get_barrier_semaphore()
    partner = device(x, y_far, 1 - h, z)
    peers = [sib, partner, to_xu, to_xd, device(x_far, y, h, z), to_zu, to_zd]
    peers += [device(x, (y + k) % NY, h, z) for k in range(1, NY)]
    for peer in peers:
        pl.semaphore_signal(barrier, inc=1, device_id=peer, device_id_type=MESH)
    pl.semaphore_wait(barrier, len(peers))

    top, low = pl.ds(0, 512), pl.ds(512, 512)
    r0 = send(root.at[top], r_all.at[seg_own, top], to_xu)
    r1 = send(root.at[low], r_all.at[seg_own, low], to_xd)
    r6 = send(root, r_all.at[seg_own], sib)

    own_panel.wait()

    def mask_into(dst_of, first_row, blocks):
        def body(i, carry):
            row = first_row + i * 128
            on = pattern[c, row // 128].astype(F32)
            value = panel_v[at(row, 128), :].astype(F32) * on
            dst_of(i, value)
            return carry

        lax.fori_loop(0, blocks, body, 0)

    def segment_row(s, yy):
        return (((s // 2) * NY + yy) * 2 + s % 2) * 256

    own_lanes, other_lanes = at((y % 2) * 128, 128), at(((y + 1) % 2) * 128, 128)
    m_copies = {}

    def over_y(i):
        s = (z + DIRECT[i]) % NZ
        for k in range(1, NY):

            def put(b, value):
                m_send[i, k - 1, at(b * 128, 128), :] = value.astype(BF)

            mask_into(put, segment_row(s, (y + k) % NY), 2)
            m_copies[i, k] = send(
                m_send.at[i, k - 1],
                m_all.at[y // 2, at(s * 256, 256), own_lanes],
                device(x, (y + k) % NY, h, z),
            )

    over_y(0)
    def own_segment(s, carry):
        def put(b, value):
            m_all[y // 2, at(s * 256 + b * 128, 128), own_lanes] = value.astype(BF)

        mask_into(put, segment_row(s, y), 2)
        return carry

    lax.fori_loop(0, 8, own_segment, 0)

    r2 = send(root.at[low], r_all.at[seg_own, low], to_xu)
    r3 = send(root.at[top], r_all.at[seg_own, top], to_xd)

    def put_transposed(b, value):
        mr_own[:, at(b * 128, 128)] = value.T.astype(BF)

    mask_into(put_transposed, z * 1024, 8)
    stays = h == y // 2

    def swap():
        return pltpu.make_async_remote_copy(
            src_ref=mr_own,
            dst_ref=mr_all.at[at((x * 2 + 1 - h) * 128, 128)],
            send_sem=swap_sems.at[0],
            recv_sem=swap_sems.at[1],
            device_id=partner,
            device_id_type=MESH,
        )

    @pl.when(stays)
    def _():
        pltpu.make_async_copy(mr_own, mr_all.at[at(seg_own * 128, 128)], swap_sems.at[1]).start()

    @pl.when(jnp.logical_not(stays))
    def _():
        swap().start()

    def slot_of(yy):
        return 2 * (yy % 2) + yy // 2

    def along_z(s, to):
        rows = at(s * 256, 256)
        refs = m_all.at[1 - y // 2, rows], m_all.at[y // 2, rows, other_lanes]
        return [send(ref, ref, to) for ref in refs]

    def arrived(copies):
        for copy in copies:
            copy.wait_recv()

    for k in range(1, NY):
        m_copies[0, k].wait_recv()
    up, down = along_z(z, to_zu), along_z(z, to_zd)
    for i in range(1, len(DIRECT)):
        over_y(i)
    own_child.wait()
    e_slot = slot_of(y)
    child_all[y] = child_v[at(e_slot * 128, 128), :]

    r0.wait_recv()
    seg_dn, seg_up, seg_far = x_dn * 2 + h, x_up * 2 + h, x_far * 2 + h
    r4 = send(r_all.at[seg_dn, top], r_all.at[seg_dn, top], to_xu)
    r1.wait_recv()
    r5 = send(r_all.at[seg_up, low], r_all.at[seg_up, low], to_xd)

    for step in range(1, Z_STEPS):
        arrived(up)
        up = along_z(wrap(z - step, NZ), to_zu)
        arrived(down)
        down = along_z(wrap(z + step, NZ), to_zd)

    r2.wait_recv()
    r7 = send(r_all.at[seg_dn], r_all.at[seg_dn], sib)
    r3.wait_recv()
    r8 = send(r_all.at[seg_up], r_all.at[seg_up], sib)

    def mr_rows(s):
        return mr_all.at[at(s * 128, 128)]

    def mr_half(s, half):
        return mr_all.at[at(s * 128 + half * 64, 64)]

    arrived(up)
    arrived(down)
    for i in range(1, len(DIRECT)):
        for k in range(1, NY):
            m_copies[i, k].wait_recv()
    child_copies = []
    for k in range(1, NY):
        yy = (y + k) % NY
        child_copies.append(
            send(child_v.at[at(slot_of(yy) * 128, 128)], child_all.at[y], device(x, yy, h, z))
        )
    own_r.wait()
    r6.wait_recv()
    r7.wait_recv()
    r8.wait_recv()

    def m_of(pair, s):
        return m_all[pair, at(s * 256, 256), :]

    def first_product(i, carry):
        pair, rows = i // 4, at((i % 4) * 256, 256)
        total = None
        for xx in (x, x_dn, x_up):
            for hh in range(2):
                s = xx * 2 + hh
                term = jnp.dot(r_all[s, rows, :], m_of(pair, s), preferred_element_type=F32)
                total = term if total is None else total + term
        prod[pair, rows, :] = total
        return carry

    lax.fori_loop(0, 4, first_product, 0)

    r4.wait_recv()
    r9 = send(r_all.at[seg_far, top], r_all.at[seg_far, top], sib)
    r5.wait_recv()
    r10 = send(r_all.at[seg_far, low], r_all.at[seg_far, low], sib)

    lax.fori_loop(4, 8, first_product, 0)
    pltpu.make_async_copy(mr_own, mr_rows(seg_own), swap_sems.at[1]).wait()
    t0 = send(mr_rows(seg_own), mr_rows(seg_own), to_xu)
    t1 = send(mr_rows(seg_own), mr_rows(seg_own), to_xd)
    t4 = send(mr_rows(seg_own), mr_rows(seg_own), sib)

    r9.wait_recv()
    r10.wait_recv()

    ycopy, zcopy = {}, {}

    def finish(pair):
        def body(quarter, carry):
            rows = at(quarter * 256, 256)
            total = prod[pair, rows, :]
            for hh in range(2):
                s = x_far * 2 + hh
                total += jnp.dot(r_all[s, rows, :], m_of(pair, s), preferred_element_type=F32)
            prod[pair, rows, :] = total
            p_send[2 * pair, rows, :] = total[:, :128].astype(BF)
            p_send[2 * pair + 1, rows, :] = total[:, 128:].astype(BF)
            return carry

        lax.fori_loop(0, 4, body, 0)

    def part(chunk, rows):
        return prod[chunk // 2, rows, pl.ds((chunk % 2) * 128, 128)]

    def half_rows(quarter, half):
        return at(quarter * 256 + half * 128, 128)

    def y_out(chunk, slot, value, to):
        y_send[chunk, slot - 4] = value.astype(BF)
        ycopy[chunk, slot] = send(y_send.at[chunk, slot - 4], y_recv.at[chunk, slot], to)

    def p_out(chunk, slot, quarter, half, to):
        ycopy[chunk, slot] = send(
            p_send.at[chunk, half_rows(quarter, half)], y_recv.at[chunk, slot], to
        )

    def stage_a(chunk):
        if chunk % 2 == 0:
            finish(chunk // 2)
        p_out(chunk, 0, y_far, 0, to_yu)
        p_out(chunk, 1, y_far, 1, to_yd)
        p_out(chunk, 2, y_up, 1, to_yu)
        p_out(chunk, 3, y_dn, 0, to_yd)

    def stage_b(chunk):
        ycopy[chunk, 0].wait_recv()
        value = part(chunk, half_rows(y_up, 0)) + y_recv[chunk, 0].astype(F32)
        y_out(chunk, 4, value, to_yu)
        ycopy[chunk, 1].wait_recv()
        value = part(chunk, half_rows(y_dn, 1)) + y_recv[chunk, 1].astype(F32)
        y_out(chunk, 5, value, to_yd)

    def o_copy(chunk, slot, quarter, half, to):
        ref = o_all.at[chunk, half_rows(quarter, half)]
        ycopy[chunk, slot] = send(ref, ref, to)

    def stage_c(chunk):
        ycopy[chunk, 3].wait_recv()
        ycopy[chunk, 4].wait_recv()
        o_all[chunk, half_rows(y, 0), :] = (
            part(chunk, half_rows(y, 0)) + y_recv[chunk, 3].astype(F32) + y_recv[chunk, 4].astype(F32)
        ).astype(BF)
        o_copy(chunk, 6, y, 0, to_yu)
        ycopy[chunk, 2].wait_recv()
        ycopy[chunk, 5].wait_recv()
        o_all[chunk, half_rows(y, 1), :] = (
            part(chunk, half_rows(y, 1)) + y_recv[chunk, 2].astype(F32) + y_recv[chunk, 5].astype(F32)
        ).astype(BF)
        o_copy(chunk, 7, y, 1, to_yd)
        o_copy(chunk, 8, y, 1, to_yu)
        o_copy(chunk, 9, y, 0, to_yd)

    def stage_d(chunk):
        ycopy[chunk, 6].wait_recv()
        o_copy(chunk, 10, y_dn, 0, to_yu)
        ycopy[chunk, 7].wait_recv()
        o_copy(chunk, 11, y_up, 1, to_yd)

    def z_out(chunk, slot, size, value, to):
        if slot % 4 == 3:
            src, dst = z_last_send.at[chunk, slot // 4], z_last_recv.at[chunk, slot // 4]
            src[...] = value
        else:
            part = pl.ds(0, size)
            src, dst = z_send.at[chunk, slot, part], z_recv.at[chunk, slot, part]
            src[...] = value.astype(BF)
        zcopy[chunk, slot] = send(src, dst, to)

    def stage_e(chunk):
        for slot in (8, 9, 10, 11):
            ycopy[chunk, slot].wait_recv()

        def body(i, carry):
            rows = at(i * 512, 512)
            d_all[chunk, rows, :] = jnp.dot(mr_all[rows, :], o_all[chunk], preferred_element_type=F32)
            return carry

        lax.fori_loop(0, 2, body, 0)
        far = ((z + 4) % NZ) * 128
        z_out(chunk, 0, 64, d_all[chunk, at(far, 64), :], to_zu)
        z_out(chunk, 4, 64, d_all[chunk, at(far + 64, 64), :], to_zd)

    def stage_f(chunk, step):
        for slot, ahead, to in ((step, 4 - step, to_zu), (4 + step, 4 + step, to_zd)):
            zcopy[chunk, slot - 1].wait_recv()
            base = ((z + ahead) % NZ) * 128
            if step == 1:
                halves = [d_all[chunk, at(base, 64), :], d_all[chunk, at(base + 64, 64), :]]
                halves[slot // 4] += z_recv[chunk, slot - 1, pl.ds(0, 64), :].astype(F32)
                value = jnp.concatenate(halves, axis=0)
            else:
                value = d_all[chunk, at(base, 128), :] + z_recv[chunk, slot - 1].astype(F32)
            z_out(chunk, slot, 128, value, to)

    e_copies, w_copies = {}, []

    def d_there(chunk):
        return pltpu.make_async_remote_copy(
            src_ref=d_send.at[chunk],
            dst_ref=d_here.at[at(e_slot * 128, 128)],
            send_sem=d_send_sems.at[chunk],
            recv_sem=d_recv_sems.at[e_slot],
            device_id=device(x, chunk, h, z),
            device_id_type=MESH,
        )

    def stage_g(chunk):
        zcopy[chunk, 3].wait_recv()
        zcopy[chunk, 7].wait_recv()
        value = d_all[chunk, at(z * 128, 128), :] + z_last_recv[chunk, 0] + z_last_recv[chunk, 1]
        value += child_all[chunk]
        ref = w_all.at[h, chunk, at(e_slot * 128, 128)]
        ref[...] = value.astype(BF)
        for k in (2, 1, 3):
            e_copies[chunk, k] = send(ref, ref, device(x, (y + k) % NY, h, z))
        d_send[chunk] = value

        @pl.when(y == chunk)
        def _():
            here = d_here.at[at(e_slot * 128, 128)]
            pltpu.make_async_copy(d_send.at[chunk], here, d_recv_sems.at[e_slot]).start()

        @pl.when(y != chunk)
        def _():
            d_there(chunk).start()

    def stage_h(chunk):
        for k in (1, 3, 2):
            e_copies[chunk, k].wait_recv()
        w_copies.append(send(w_all.at[h, chunk], w_all.at[h, chunk], sib))

    stages = [stage_a, stage_b, stage_c, stage_d, stage_e]
    stages += [functools.partial(stage_f, step=step) for step in (1, 2, 3)]
    stages += [stage_g, stage_h]
    for step in range(len(stages) + NY - 1):
        order = [chunk for chunk in range(NY) if 0 <= step - chunk < len(stages)]
        if step == 2:
            t0.wait_recv()
            t2 = send(mr_half(seg_dn, 0), mr_half(seg_dn, 0), to_xu)
            t5 = send(mr_rows(seg_dn), mr_rows(seg_dn), sib)
            t1.wait_recv()
            t3 = send(mr_half(seg_up, 1), mr_half(seg_up, 1), to_xd)
            t6 = send(mr_rows(seg_up), mr_rows(seg_up), sib)
        if step == 8:
            for copy in child_copies:
                copy.wait_recv()
        if step == 4:
            t2.wait_recv()
            t3.wait_recv()
            t7 = send(mr_rows(seg_far), mr_rows(seg_far), sib)
            order = [k for k in (1, 2, 3, 0) if step - k < len(stages)]
        for chunk in order:
            if step == 4 and chunk == 0:
                for copy in (t4, t5, t6, t7):
                    copy.wait_recv()
            stages[step - chunk](chunk)

    def candidate(xx):
        t = owner[(xx * NY + y) * 2 + h]
        on = (t // (2 * NY) == x).astype(F32)
        return w_all[t % 2, (t // 2) % NY].astype(F32) * on

    for copy in w_copies:
        copy.wait_recv()
    x_copies = []
    for k in (2, 1, 3):
        xx = (x + k) % NX
        x_send[k] = candidate(xx).astype(BF)
        x_copies.append(send(x_send.at[k], x_recv.at[k], device(xx, y, h, z)))
    off_out[...] = o_all[y]
    for slot in range(4):
        ref = d_here.at[pl.ds(slot * 128, 128)]
        pltpu.make_async_copy(ref, ref, d_recv_sems.at[slot]).wait()
    diag_out[...] = d_here[...]
    own_out[...] = candidate(x).astype(BF)
    for copy in x_copies:
        copy.wait_recv()

    def add_up(i, carry):
        rows = at(i * 128, 128)
        total = own_out[rows, :].astype(F32)
        for k in (1, 2, 3):
            total += x_recv[k, rows, :].astype(F32)
        own_out[rows, :] = total.astype(BF)
        return carry

    lax.fori_loop(0, 4, add_up, 0)

    links.drain()
    for chunk in range(NY):

        @pl.when(y != chunk)
        def _(chunk=chunk):
            d_there(chunk).wait_send()

    @pl.when(jnp.logical_not(stays))
    def _():
        swap().wait_send()


def outputs(off, diag, own, off_out, diag_out, own_out):
    off_out[...] = -off[...].astype(F32)
    diag_out[...] = diag[...]
    for i in range(4):
        rows = pl.ds(i * 128, 128)
        own_out[:, rows] = own[rows, :].astype(F32).T.astype(BF)


def on_device(root_inv, panel, pattern, child_diag, owner):
    vmem = pl.BlockSpec(memory_space=pltpu.VMEM)
    smem = pl.BlockSpec(memory_space=pltpu.SMEM)
    hbm = pl.BlockSpec(memory_space=pl.ANY)
    off, diag, own = pl.pallas_call(
        kernel,
        out_shape=(
            jax.ShapeDtypeStruct((1024, 128), BF),
            jax.ShapeDtypeStruct((512, 128), F32),
            jax.ShapeDtypeStruct((512, 128), BF),
        ),
        in_specs=[hbm, hbm, smem, hbm, smem],
        out_specs=(vmem, vmem, vmem),
        scratch_shapes=[
            pltpu.VMEM((8, 1024, 256), BF),
            pltpu.VMEM((8192, 128), BF),
            pltpu.VMEM((len(DIRECT), NY - 1, 256, 128), BF),
            pltpu.VMEM((2, 2048, 256), BF),
            pltpu.VMEM((128, 1024), BF),
            pltpu.VMEM((1024, 1024), BF),
            pltpu.VMEM((512, 128), F32),
            pltpu.VMEM((NY, 128, 128), F32),
            pltpu.VMEM((2, 1024, 256), F32),
            pltpu.VMEM((NY, 1024, 128), BF),
            pltpu.VMEM((NY, 2, 128, 128), BF),
            pltpu.VMEM((NY, 6, 128, 128), BF),
            pltpu.VMEM((NY, 1024, 128), BF),
            pltpu.VMEM((NY, 1024, 128), F32),
            pltpu.VMEM((NY, 7, 128, 128), BF),
            pltpu.VMEM((NY, 7, 128, 128), BF),
            pltpu.VMEM((NY, 2, 128, 128), F32),
            pltpu.VMEM((NY, 2, 128, 128), F32),
            pltpu.VMEM((NY, 128, 128), F32),
            pltpu.VMEM((512, 128), F32),
            pltpu.VMEM((2, NY, 512, 128), BF),
            pltpu.VMEM((NX, 512, 128), BF),
            pltpu.VMEM((NX, 512, 128), BF),
            pltpu.SemaphoreType.DMA((N_LINKS,)),
            pltpu.SemaphoreType.DMA((N_LINKS,)),
            pltpu.SemaphoreType.DMA((2,)),
            pltpu.SemaphoreType.DMA((NY,)),
            pltpu.SemaphoreType.DMA((4,)),
            pltpu.SemaphoreType.DMA((3,)),
        ],
        compiler_params=pltpu.CompilerParams(
            collective_id=0, has_side_effects=True, vmem_limit_bytes=60 * 1024 * 1024
        ),
    )(root_inv, panel, pattern.T, child_diag, owner)
    return pl.pallas_call(
        outputs,
        out_shape=(
            jax.ShapeDtypeStruct((1024, 128), F32),
            jax.ShapeDtypeStruct((512, 128), F32),
            jax.ShapeDtypeStruct((128, 512), BF),
        ),
        in_specs=[vmem] * 3,
        out_specs=(vmem,) * 3,
        compiler_params=pltpu.CompilerParams(vmem_limit_bytes=60 * 1024 * 1024),
    )(off, diag, own)


def solution(mesh):
    placed = (P("row", "col"), P(None, "col"), P(), P("row", "col"), P())
    return jax.shard_map(
        on_device,
        mesh=mesh,
        in_specs=placed,
        out_specs=(P("row", "col"), P("row", "col"), P("col", "row")),
        check_vma=False,
    )
```

time: 119 us -> 96.5 us (0.81)
  Pallas kernels: 111 us -> 95.6 us
  local copies, waits for them, and re-layouts: 6.51 us -> 0 us
    pallas_call x1, Pallas kernels: 111 us -> 93.6 us  [on_device(): pl.pallas_call(kernel, out_shape=(jax.ShapeDtypeStruct((1024, 128), BF),...]
    unnamed x11 -> x0, local copies, waits for them, and re-layouts: 6.51 us -> none
    pallas_call x0 -> x1, Pallas kernels: none -> 2.01 us  [on_device(): pl.pallas_call(outputs, out_shape=(jax.ShapeDtypeStruct((1024, 128), F32)...]
where the time goes in v2:
time: 96.5 us; the launch traced here: 96.3 us
  Pallas kernels  95.6 us (99%)
    pallas_call x1, Pallas kernels, on_device(): pl.pallas_call(kernel, out_shape=(jax.ShapeDtypeStruct((1024, 128), BF),...  93.6 us
    pallas_call x1, Pallas kernels, on_device(): pl.pallas_call(outputs, out_shape=(jax.ShapeDtypeStruct((1024, 128), F32)...  2.01 us

profile of v2, /device:TPU:1, one launch (start us, length us, event | category | flops | bytes accessed | tf_op | source)
XLA Modules:
  0.0 96.3 jit_solution(16850125414284298175)
XLA Ops:
  0.6 93.6 %shard_map.76 = (bf16[1024,128]{1,0:T(8,128)(2,1)}, f32[512,128]{1,0:T(8,128)}, bf16[512,128]{1,0:T(8,128)(2,1)}) custom-call(bf16[1024,256]{1,0:T(8,128)(2,1)} %root.1, bf16[8192,128]{1,0:T(8,128)(2,1)} %panel.1, s32[32,64]{1,0:T(8,128)} %bitcast.1, f32[512,128]{1,0:T(8,128)} %child.1, s32[32]{0:T(128)} %owner.1), custom_call_target="tpu_custom_call" | custom-call | tf_op jit(solution)/shard_map/pallas_call | solution.py:490
  94.3 2.0 %shard_map.77 = (f32[1024,128]{1,0:T(8,128)}, f32[512,128]{1,0:T(8,128)}, bf16[128,512]{1,0:T(8,128)(2,1)}) custom-call(bf16[1024,128]{1,0:T(8,128)(2,1)} %get-tuple-element.6.off, f32[512,128]{1,0:T(8,128)} %get-tuple-element.7.diag, bf16[512,128]{1,0:T(8,128)(2,1)} %get-tuple-element.8.own), custom_call_target="tpu_custom_call" | custom-call | tf_op jit(solution)/shard_map/pallas_call | solution.py:534

commit v3 on v2

--- a/solution.py
+++ b/solution.py
@@ -54,7 +54,7 @@
     off_out, diag_out, own_out,
     r_all, panel_v, m_send, m_all, mr_own, mr_all, child_v, child_all,
     prod, p_send, y_send, y_recv, o_all, d_all, z_send, z_recv, z_last_send, z_last_recv,
-    d_send, d_here, w_all, x_send, x_recv,
+    d_send, d_here, w_all, last_send, own_all,
     send_sems, recv_sems, swap_sems, d_send_sems, d_recv_sems, local_sems,
 ):
     z = lax.axis_index("row")
@@ -162,21 +162,13 @@
             device_id_type=MESH,
         )
 
-    @pl.when(stays)
-    def _():
-        pltpu.make_async_copy(mr_own, mr_all.at[at(seg_own * 128, 128)], swap_sems.at[1]).start()
-
-    @pl.when(jnp.logical_not(stays))
-    def _():
-        swap().start()
-
     def slot_of(yy):
         return 2 * (yy % 2) + yy // 2
 
-    def along_z(s, to):
+    def along_z(s, i, to):
         rows = at(s * 256, 256)
-        refs = m_all.at[1 - y // 2, rows], m_all.at[y // 2, rows, other_lanes]
-        return [send(ref, ref, to) for ref in refs]
+        ref = m_all.at[y // 2, rows, other_lanes] if i == 0 else m_all.at[1 - y // 2, rows]
+        return send(ref, ref, to)
 
     def arrived(copies):
         for copy in copies:
@@ -184,7 +176,10 @@
 
     for k in range(1, NY):
         m_copies[0, k].wait_recv()
-    up, down = along_z(z, to_zu), along_z(z, to_zd)
+    up, down = [], []
+    for i in range(2):
+        up.append(along_z(z, i, to_zu))
+        down.append(along_z(z, i, to_zd))
     for i in range(1, len(DIRECT)):
         over_y(i)
     own_child.wait()
@@ -198,10 +193,11 @@
     r5 = send(r_all.at[seg_up, low], r_all.at[seg_up, low], to_xd)
 
     for step in range(1, Z_STEPS):
-        arrived(up)
-        up = along_z(wrap(z - step, NZ), to_zu)
-        arrived(down)
-        down = along_z(wrap(z + step, NZ), to_zd)
+        for i in range(2):
+            up[i].wait_recv()
+            up[i] = along_z(wrap(z - step, NZ), i, to_zu)
+            down[i].wait_recv()
+            down[i] = along_z(wrap(z + step, NZ), i, to_zd)
 
     r2.wait_recv()
     r7 = send(r_all.at[seg_dn], r_all.at[seg_dn], sib)
@@ -213,6 +209,14 @@
 
     def mr_half(s, half):
         return mr_all.at[at(s * 128 + half * 64, 64)]
+
+    @pl.when(stays)
+    def _():
+        pltpu.make_async_copy(mr_own, mr_all.at[at(seg_own * 128, 128)], swap_sems.at[1]).start()
+
+    @pl.when(jnp.logical_not(stays))
+    def _():
+        swap().start()
 
     arrived(up)
     arrived(down)
@@ -347,15 +351,15 @@
         for slot in (8, 9, 10, 11):
             ycopy[chunk, slot].wait_recv()
 
-        def body(i, carry):
+        def multiply(i):
             rows = at(i * 512, 512)
             d_all[chunk, rows, :] = jnp.dot(mr_all[rows, :], o_all[chunk], preferred_element_type=F32)
-            return carry
-
-        lax.fori_loop(0, 2, body, 0)
-        far = ((z + 4) % NZ) * 128
-        z_out(chunk, 0, 64, d_all[chunk, at(far, 64), :], to_zu)
-        z_out(chunk, 4, 64, d_all[chunk, at(far + 64, 64), :], to_zd)
+
+        far = (z + 4) % NZ
+        multiply(far // 4)
+        z_out(chunk, 0, 64, d_all[chunk, at(far * 128, 64), :], to_zu)
+        z_out(chunk, 4, 64, d_all[chunk, at(far * 128 + 64, 64), :], to_zd)
+        multiply(1 - far // 4)
 
     def stage_f(chunk, step):
         for slot, ahead, to in ((step, 4 - step, to_zu), (4 + step, 4 + step, to_zd)):
@@ -386,10 +390,10 @@
         zcopy[chunk, 7].wait_recv()
         value = d_all[chunk, at(z * 128, 128), :] + z_last_recv[chunk, 0] + z_last_recv[chunk, 1]
         value += child_all[chunk]
-        ref = w_all.at[h, chunk, at(e_slot * 128, 128)]
+        ref = w_all.at[h, chunk, x]
         ref[...] = value.astype(BF)
         for k in (2, 1, 3):
-            e_copies[chunk, k] = send(ref, ref, device(x, (y + k) % NY, h, z))
+            e_copies[chunk, k] = send(ref, ref, device((x + k) % NX, y, h, z))
         d_send[chunk] = value
 
         @pl.when(y == chunk)
@@ -411,6 +415,8 @@
     stages += [stage_g, stage_h]
     for step in range(len(stages) + NY - 1):
         order = [chunk for chunk in range(NY) if 0 <= step - chunk < len(stages)]
+        if step >= NY:
+            order = order[::-1]
         if step == 2:
             t0.wait_recv()
             t2 = send(mr_half(seg_dn, 0), mr_half(seg_dn, 0), to_xu)
@@ -425,43 +431,34 @@
             t2.wait_recv()
             t3.wait_recv()
             t7 = send(mr_rows(seg_far), mr_rows(seg_far), sib)
-            order = [k for k in (1, 2, 3, 0) if step - k < len(stages)]
         for chunk in order:
             if step == 4 and chunk == 0:
                 for copy in (t4, t5, t6, t7):
                     copy.wait_recv()
             stages[step - chunk](chunk)
 
-    def candidate(xx):
-        t = owner[(xx * NY + y) * 2 + h]
-        on = (t // (2 * NY) == x).astype(F32)
-        return w_all[t % 2, (t // 2) % NY].astype(F32) * on
-
     for copy in w_copies:
         copy.wait_recv()
-    x_copies = []
+    own_rows = own_all.at[at(e_slot * 128, 128)]
+
+    def owned_by(yy):
+        t = owner[(x * NY + yy) * 2 + h]
+        return w_all[t % 2, (t // 2) % NY, t // (2 * NY)]
+
+    last_copies = []
     for k in (2, 1, 3):
-        xx = (x + k) % NX
-        x_send[k] = candidate(xx).astype(BF)
-        x_copies.append(send(x_send.at[k], x_recv.at[k], device(xx, y, h, z)))
+        yy = (y + k) % NY
+        last_send[k - 1] = owned_by(yy)
+        last_copies.append(send(last_send.at[k - 1], own_rows, device(x, yy, h, z)))
+    own_rows[...] = owned_by(y)
     off_out[...] = o_all[y]
     for slot in range(4):
         ref = d_here.at[pl.ds(slot * 128, 128)]
         pltpu.make_async_copy(ref, ref, d_recv_sems.at[slot]).wait()
     diag_out[...] = d_here[...]
-    own_out[...] = candidate(x).astype(BF)
-    for copy in x_copies:
+    for copy in last_copies:
         copy.wait_recv()
-
-    def add_up(i, carry):
-        rows = at(i * 128, 128)
-        total = own_out[rows, :].astype(F32)
-        for k in (1, 2, 3):
-            total += x_recv[k, rows, :].astype(F32)
-        own_out[rows, :] = total.astype(BF)
-        return carry
-
-    lax.fori_loop(0, 4, add_up, 0)
+    own_out[...] = own_all[...]
 
     links.drain()
     for chunk in range(NY):
@@ -517,9 +514,9 @@
             pltpu.VMEM((NY, 2, 128, 128), F32),
             pltpu.VMEM((NY, 128, 128), F32),
             pltpu.VMEM((512, 128), F32),
-            pltpu.VMEM((2, NY, 512, 128), BF),
-            pltpu.VMEM((NX, 512, 128), BF),
-            pltpu.VMEM((NX, 512, 128), BF),
+            pltpu.VMEM((2, NY, NX, 128, 128), BF),
+            pltpu.VMEM((NY - 1, 128, 128), BF),
+            pltpu.VMEM((512, 128), BF),
             pltpu.SemaphoreType.DMA((N_LINKS,)),
             pltpu.SemaphoreType.DMA((N_LINKS,)),
             pltpu.SemaphoreType.DMA((2,)),

time: 96.5 us -> 90.3 us (0.936)
  Pallas kernels: 95.6 us -> 89.5 us
    pallas_call x1, Pallas kernels: 93.6 us -> 87.5 us  [on_device(): pl.pallas_call(kernel, out_shape=(jax.ShapeDtypeStruct((1024, 128), BF),...]
where the time goes in v3:
time: 90.3 us; the launch traced here: 90.1 us
  Pallas kernels  89.5 us (99%)
    pallas_call x1, Pallas kernels, on_device(): pl.pallas_call(kernel, out_shape=(jax.ShapeDtypeStruct((1024, 128), BF),...  87.5 us
    pallas_call x1, Pallas kernels, on_device(): pl.pallas_call(outputs, out_shape=(jax.ShapeDtypeStruct((1024, 128), F32)...  2.01 us

profile of v3, /device:TPU:1, one launch (start us, length us, event | category | flops | bytes accessed | tf_op | source)
XLA Modules:
  0.0 90.1 jit_solution(2039251191351533253)
XLA Ops:
  0.6 87.5 %shard_map.76 = (bf16[1024,128]{1,0:T(8,128)(2,1)}, f32[512,128]{1,0:T(8,128)}, bf16[512,128]{1,0:T(8,128)(2,1)}) custom-call(bf16[1024,256]{1,0:T(8,128)(2,1)} %root.1, bf16[8192,128]{1,0:T(8,128)(2,1)} %panel.1, s32[32,64]{1,0:T(8,128)} %bitcast.1, f32[512,128]{1,0:T(8,128)} %child.1, s32[32]{0:T(128)} %owner.1), custom_call_target="tpu_custom_call" | custom-call | tf_op jit(solution)/shard_map/pallas_call | solution.py:487
  88.1 2.0 %shard_map.77 = (f32[1024,128]{1,0:T(8,128)}, f32[512,128]{1,0:T(8,128)}, bf16[128,512]{1,0:T(8,128)(2,1)}) custom-call(bf16[1024,128]{1,0:T(8,128)(2,1)} %get-tuple-element.6.off, f32[512,128]{1,0:T(8,128)} %get-tuple-element.7.diag, bf16[512,128]{1,0:T(8,128)(2,1)} %get-tuple-element.8.own), custom_call_target="tpu_custom_call" | custom-call | tf_op jit(solution)/shard_map/pallas_call | solution.py:531

commit v4 on v3

--- a/solution.py
+++ b/solution.py
@@ -415,7 +415,7 @@
     stages += [stage_g, stage_h]
     for step in range(len(stages) + NY - 1):
         order = [chunk for chunk in range(NY) if 0 <= step - chunk < len(stages)]
-        if step >= NY:
+        if step >= 3:
             order = order[::-1]
         if step == 2:
             t0.wait_recv()

time: 90.3 us -> 89.6 us (level)
  no operation moved by 1% of the time
where the time goes in v4:
time: 89.6 us; the launch traced here: 89.5 us
  Pallas kernels  88.8 us (99%)
    pallas_call x1, Pallas kernels, on_device(): pl.pallas_call(kernel, out_shape=(jax.ShapeDtypeStruct((1024, 128), BF),...  86.8 us
    pallas_call x1, Pallas kernels, on_device(): pl.pallas_call(outputs, out_shape=(jax.ShapeDtypeStruct((1024, 128), F32)...  2.01 us

profile of v4, /device:TPU:1, one launch (start us, length us, event | category | flops | bytes accessed | tf_op | source)
XLA Modules:
  0.0 89.5 jit_solution(12345194702059109095)
XLA Ops:
  0.6 86.8 %shard_map.76 = (bf16[1024,128]{1,0:T(8,128)(2,1)}, f32[512,128]{1,0:T(8,128)}, bf16[512,128]{1,0:T(8,128)(2,1)}) custom-call(bf16[1024,256]{1,0:T(8,128)(2,1)} %root.1, bf16[8192,128]{1,0:T(8,128)(2,1)} %panel.1, s32[32,64]{1,0:T(8,128)} %bitcast.1, f32[512,128]{1,0:T(8,128)} %child.1, s32[32]{0:T(128)} %owner.1), custom_call_target="tpu_custom_call" | custom-call | tf_op jit(solution)/shard_map/pallas_call | solution.py:487
  87.4 2.0 %shard_map.77 = (f32[1024,128]{1,0:T(8,128)}, f32[512,128]{1,0:T(8,128)}, bf16[128,512]{1,0:T(8,128)(2,1)}) custom-call(bf16[1024,128]{1,0:T(8,128)(2,1)} %get-tuple-element.6.off, f32[512,128]{1,0:T(8,128)} %get-tuple-element.7.diag, bf16[512,128]{1,0:T(8,128)(2,1)} %get-tuple-element.8.own), custom_call_target="tpu_custom_call" | custom-call | tf_op jit(solution)/shard_map/pallas_call | solution.py:531

commit v5 on v4

--- a/solution.py
+++ b/solution.py
@@ -217,6 +217,11 @@
     @pl.when(jnp.logical_not(stays))
     def _():
         swap().start()
+
+    r4.wait_recv()
+    r9 = send(r_all.at[seg_far, top], r_all.at[seg_far, top], sib)
+    r5.wait_recv()
+    r10 = send(r_all.at[seg_far, low], r_all.at[seg_far, low], sib)
 
     arrived(up)
     arrived(down)
@@ -249,11 +254,6 @@
         return carry
 
     lax.fori_loop(0, 4, first_product, 0)
-
-    r4.wait_recv()
-    r9 = send(r_all.at[seg_far, top], r_all.at[seg_far, top], sib)
-    r5.wait_recv()
-    r10 = send(r_all.at[seg_far, low], r_all.at[seg_far, low], sib)
 
     lax.fori_loop(4, 8, first_product, 0)
     pltpu.make_async_copy(mr_own, mr_rows(seg_own), swap_sems.at[1]).wait()

time: 89.6 us -> 89.7 us (level)
  no operation moved by 1% of the time
where the time goes in v5:
time: 89.7 us; the launch traced here: 89.5 us
  Pallas kernels  88.8 us (99%)
    pallas_call x1, Pallas kernels, on_device(): pl.pallas_call(kernel, out_shape=(jax.ShapeDtypeStruct((1024, 128), BF),...  86.8 us
    pallas_call x1, Pallas kernels, on_device(): pl.pallas_call(outputs, out_shape=(jax.ShapeDtypeStruct((1024, 128), F32)...  2.01 us

profile of v5, /device:TPU:1, one launch (start us, length us, event | category | flops | bytes accessed | tf_op | source)
XLA Modules:
  0.0 89.5 jit_solution(1525827393045418131)
XLA Ops:
  0.6 86.8 %shard_map.76 = (bf16[1024,128]{1,0:T(8,128)(2,1)}, f32[512,128]{1,0:T(8,128)}, bf16[512,128]{1,0:T(8,128)(2,1)}) custom-call(bf16[1024,256]{1,0:T(8,128)(2,1)} %root.1, bf16[8192,128]{1,0:T(8,128)(2,1)} %panel.1, s32[32,64]{1,0:T(8,128)} %bitcast.1, f32[512,128]{1,0:T(8,128)} %child.1, s32[32]{0:T(128)} %owner.1), custom_call_target="tpu_custom_call" | custom-call | tf_op jit(solution)/shard_map/pallas_call | solution.py:487
  87.5 2.0 %shard_map.77 = (f32[1024,128]{1,0:T(8,128)}, f32[512,128]{1,0:T(8,128)}, bf16[128,512]{1,0:T(8,128)(2,1)}) custom-call(bf16[1024,128]{1,0:T(8,128)(2,1)} %get-tuple-element.6.off, f32[512,128]{1,0:T(8,128)} %get-tuple-element.7.diag, bf16[512,128]{1,0:T(8,128)(2,1)} %get-tuple-element.8.own), custom_call_target="tpu_custom_call" | custom-call | tf_op jit(solution)/shard_map/pallas_call | solution.py:531
